TPU v7x, 32 devices: a whole 2x2x4 slice. The times are simulated.
32 devices in a mesh: rep: 8 (over y, x, core), sp: 4 (over z).
Axes of the slice: x: 2, y: 2, z: 4, core: 2. Of those that a mesh axis runs over, the one named last changes fastest.
Arguments:
- positions: float32 [8, 3, 32768], P('rep', None, 'sp'), may hold values from -18 to 18
- velocities: float32 [8, 3, 32768], P('rep', None, 'sp'), may hold values from -6 to 6
- strength: float32 [8, 32768], P('rep', 'sp'), may hold values from 0.5 to 2
- inv_mass: float32 [8, 32768], P('rep', 'sp'), may hold values from 0.1 to 1
- tile_lists: int32 [8, 4, 256, 4], P('rep', None, 'sp'), may hold values from 0 to 127, as said below
- solute_index: int32 [8, 1024], P('rep', 'sp'), may hold values from 0 to 8191, as said below
- scatter_weight: float32 [8, 1024], P('rep', 'sp'), may hold values from 0.3 to 3
- intensity_exp: float32 [48], replicated, may hold values from 0.5 to 3
- precision: float32 [48], replicated, may hold values from 1 to 4
Outputs:
- positions_out: float32 [8, 3, 32768], P('rep', None, 'sp')
- velocities_out: float32 [8, 3, 32768], P('rep', None, 'sp')
Inputs may be any that keep to these rules, and one draw needn't show every extreme that they name: `tile_lists`: for each replica, step and local block b of a domain (numbered 0 to 63), the 4 entries are distinct extended block numbers from b to b + 64, among them b, b + 32 and b + 64. `solute_index`: within each replica and domain the 256 entries are distinct local atom numbers.
All inputs are finite; a program needn't handle non-finite values.
Results may differ from a plain program's by a relative error of at most 0.0001.
Values sent between devices are 32-bit elements; how exact they have to be, the bound alone decides.
A program may use at most 128 MiB of HBM per device.

v0:
```python
import math

import jax
import jax.numpy as jnp
from jax import lax
from jax.sharding import PartitionSpec as P

M = 784
OUTER = 2
INNER = 2


TIME_STEP = 0.05
PAIR_STRENGTH = 0.2
HALF_INVERSE = 0.03125
shell_batch = 8
group_limit = 8


def extended_2(cells, sides, width):
    for axis, dim in sides:
        count = lax.axis_size(axis)
        ends = count - 1
        head = lax.slice_in_dim(cells, 0, width, axis=dim)
        tail = lax.slice_in_dim(cells, cells.shape[dim] - width, cells.shape[dim], axis=dim)
        cells = jnp.concatenate(
            [
                lax.ppermute(tail, axis, [(i, (i + 1) % count) for i in range(ends)]),
                cells,
                lax.ppermute(head, axis, [((i + 1) % count, i) for i in range(ends)]),
            ],
            axis=dim,
        )
    return cells


def directions(total_terms):
    order_index = jnp.arange(total_terms, dtype=jnp.int32)
    height = 1.0 - (2.0 * order_index.astype(jnp.float32) + 1.0) / total_terms
    radius = jnp.sqrt(1.0 - height * height)
    azimuth = (order_index * 610 % 987).astype(jnp.float32) * (2.0 * math.pi / 987.0)
    return (radius * jnp.cos(azimuth), radius * jnp.sin(azimuth), height)


def shell_values(total_shells):
    return 1.0 + 3.0 * jnp.arange(total_shells, dtype=jnp.int32).astype(jnp.float32) / total_shells


def projection(points, dir_x, dir_y, dir_z):
    return (
        dir_x[:, None] * points[0][None, :]
        + dir_y[:, None] * points[1][None, :]
        + dir_z[:, None] * points[2][None, :]
    )


def amplitude_terms(project, weights, shell_q):
    shell_blocks = shell_q.reshape(-1, shell_batch)

    def one_block(shell_block):
        phases = shell_block[:, None, None] * project[None]
        return jnp.stack(
            [
                jnp.sum(weights * jnp.cos(phases), axis=-1),
                jnp.sum(weights * jnp.sin(phases), axis=-1),
            ]
        )

    result = lax.map(one_block, shell_blocks)
    return jnp.transpose(result, (1, 0, 2, 3)).reshape(2, -1, project.shape[0])


def shell_intensity(amplitude):
    return jnp.mean(amplitude[0] * amplitude[0] + amplitude[1] * amplitude[1], axis=-1)


def scale_grad(amplitude, intensity, precision, intensity_exp, total_terms):
    coef_shell = 2.0 * precision * (intensity - intensity_exp) / total_terms
    return coef_shell[None, :, None] * amplitude


def restraint_forces(project, weights, shell_q, weight_grad, dir_x, dir_y, dir_z):
    shell_blocks = shell_q.reshape(-1, shell_batch)
    grad_real = weight_grad[0].reshape(-1, shell_batch, project.shape[0])
    grad_imag = weight_grad[1].reshape(-1, shell_batch, project.shape[0])

    def add_block(running, pieces):
        shell_block, block_real, block_imag = pieces
        phases = shell_block[:, None, None] * project[None]
        block_term = jnp.sum(
            shell_block[:, None, None]
            * (block_imag[:, :, None] * jnp.cos(phases) - block_real[:, :, None] * jnp.sin(phases)),
            axis=0,
        )
        return (running + block_term, None)

    running, unused = lax.scan(
        add_block, jnp.zeros(project.shape, jnp.float32), (shell_blocks, grad_real, grad_imag)
    )
    return jnp.stack(
        [
            -weights * jnp.sum(dir_x[:, None] * running, axis=0),
            -weights * jnp.sum(dir_y[:, None] * running, axis=0),
            -weights * jnp.sum(dir_z[:, None] * running, axis=0),
        ]
    )


def pair_group(own_rows, near_rows, coupling):
    delta_list = [
        own_rows[component][:, :, None] - near_rows[component][:, None, :] for component in range(3)
    ]
    distance = (
        delta_list[0] * delta_list[0]
        + delta_list[1] * delta_list[1]
        + delta_list[2] * delta_list[2]
    )
    pair_weight = (
        coupling
        * own_rows[3][:, :, None]
        * near_rows[3][:, None, :]
        * jnp.exp(-HALF_INVERSE * distance)
    )
    return jnp.stack([jnp.sum(pair_weight * delta, axis=-1) for delta in delta_list])


def pair_forces(own_blocks, ext_blocks, tile_list):
    block_count, neighbours = tile_list.shape
    block_width = own_blocks.shape[2]
    group_size = min(group_limit, block_count)
    coupling = PAIR_STRENGTH / math.sqrt(neighbours * block_width)
    nearby = jnp.take(ext_blocks, tile_list.reshape(-1), axis=1).reshape(
        4, block_count // group_size, group_size, neighbours * block_width
    )
    grouped = own_blocks.reshape(4, block_count // group_size, group_size, block_width)

    def one_group(pieces):
        return pair_group(pieces[0], pieces[1], coupling)

    result = lax.map(one_group, (jnp.moveaxis(grouped, 1, 0), jnp.moveaxis(nearby, 1, 0)))
    return jnp.moveaxis(result, 0, 1).reshape(3, -1)


def shards(
    positions,
    velocities,
    strength,
    inv_mass,
    tile_lists,
    solute_index,
    scatter_weight,
    intensity_exp,
    precision,
):
    coords_now = positions[0]
    speed_now = velocities[0]
    charge = strength[0]
    inverse = inv_mass[0]
    solute_slots = solute_index[0]
    weights = scatter_weight[0]
    atom_dev = coords_now.shape[1]
    rim_width = atom_dev // 2
    block_width = 128
    replica_count = lax.axis_size("rep")
    scale_norm = 1.0 / math.sqrt(lax.axis_size("sp") * solute_slots.shape[0])
    dir_x, dir_y, dir_z = directions(M)
    shell_q = shell_values(intensity_exp.shape[0])
    mass_here = inverse[solute_slots]
    charge_ext = extended_2(charge[None, :], (("sp", 1),), rim_width)
    for outer_step in range(OUTER):
        points = jnp.take(coords_now, solute_slots, axis=1)
        project = projection(points, dir_x, dir_y, dir_z)
        partial_value = amplitude_terms(project, weights, shell_q) * scale_norm
        amplitude = lax.psum(partial_value, "sp")
        intensity = lax.psum(shell_intensity(amplitude), "rep") / replica_count
        weight_grad = scale_grad(amplitude, intensity, precision, intensity_exp, M)
        saxs_kick = restraint_forces(project, weights, shell_q, weight_grad, dir_x, dir_y, dir_z)
        for inner_step in range(INNER):
            tile_list = tile_lists[0, outer_step * INNER + inner_step]
            rows_all = jnp.concatenate([coords_now, charge[None, :]], axis=0)
            coords_ext = extended_2(coords_now, (("sp", 1),), rim_width)
            extended = jnp.concatenate([coords_ext, charge_ext], axis=0)
            own_blocks = rows_all.reshape(4, atom_dev // block_width, block_width)
            ext_blocks = extended.reshape(4, extended.shape[1] // block_width, block_width)
            pair_push = pair_forces(own_blocks, ext_blocks, tile_list)
            speed_now = speed_now + TIME_STEP * inverse[None, :] * pair_push
            coords_now = coords_now + TIME_STEP * speed_now
        impulse = INNER * TIME_STEP * mass_here[None, :] * saxs_kick
        speed_now = speed_now.at[:, solute_slots].add(impulse)
    return (coords_now[None], speed_now[None])


def solution(mesh):
    in_specs = (
        P("rep", None, "sp"),
        P("rep", None, "sp"),
        P("rep", "sp"),
        P("rep", "sp"),
        P("rep", None, "sp", None),
        P("rep", "sp"),
        P("rep", "sp"),
        P(),
        P(),
    )
    out_specs = (P("rep", None, "sp"), P("rep", None, "sp"))
    return jax.shard_map(shards, mesh=mesh, in_specs=in_specs, out_specs=out_specs, check_vma=False)
```

profile of v0, /device:TPU:0, one launch (start us, length us, event | category | flops | bytes accessed | tf_op | source)
XLA Modules:
  0.0 836.7 jit_solution(17175349959949539075)
XLA Ops:
  39.1 16.6 %while.84 = (s32[]{:T(128)}, f32[8,3,8,128]{3,2,1,0:T(8,128)S(1)}, f32[8,4,8,128]{3,2,0,1:T(8,128)S(1)}, f32[8,4,8,512]{3,2,0,1:T(8,128)S(1)}, s32[]{:T(128)}) while((s32[]{:T(128)}, f32[8,3,8,128]{3,2,1,0:T(8,128)S(1)}, f32[8,4,8,128]{3,2,0,1:T(8,128)S(1)}, f32[8,4,8,512]{3,2,0,1:T(8,128)S(1)}, s32[]{:T(128)}) %tuple.299), condition=%wide.region_4.6_spmd, body=%wide.region_0.5_spmd.sunk | while | flops 8916994 | bytes 446537 | solution.py:140
  68.4 21.4 %while.85 = (s32[]{:T(128)}, f32[8,3,8,128]{3,2,1,0:T(8,128)S(1)}, f32[8,4,8,128]{3,2,1,0:T(8,128)}, f32[8,4,8,512]{3,2,0,1:T(8,128)S(1)}, s32[]{:T(128)}, /*index=5*/s32[]{:T(128)}, s32[]{}, s32[]{}, s32[]{}) while((s32[]{:T(128)}, f32[8,3,8,128]{3,2,1,0:T(8,128)S(1)}, f32[8,4,8,128]{3,2,1,0:T(8,128)}, f32[8,4,8,512]{3,2,0,1:T(8,128)S(1)}, ...), condition=%wide.region_9.11_spmd, body=%wide.region_5.10_spmd.sunk | while | flops 8916997 | bytes 413849 | solution.py:140
  96.2 154.6 %while.89 = (s32[]{:T(128)}, f32[6,2,8,784]{3,2,0,1:T(8,128)S(1)}, f32[1,256]{1,0:T(1,128)S(1)}, f32[6,8]{1,0:T(8,128)}, f32[256]{0:T(256)S(1)}, /*index=5*/f32[...) while((s32[]{:T(128)}, f32[6,2,8,784]{3,2,0,1:T(8,128)S(1)}, ...), condition=%wide.region_37.40_spmd.clone, body=%wide.region_34.39_spmd.clone.sunk | while | flops 9031682 | bytes 1784213 | solution.py:69
  97.3 24.6 %fusion.152 = (f32[8,784]{1,0:T(8,128)S(1)}, f32[8,784]{1,0:T(8,128)S(1)}) fusion(f32[784,256]{1,0:T(8,128)S(1)} %multiply_add_fusion.13, f32[8]{0:T(128)S(1)} %fusion.151, f32[256]{0:T(256)S(1)} %bitcast.427), kind=kLoop, calls=%fused_computation.132.clone.1 | loop fusion | flops 8015616 | bytes 854048 | tf_op jit(solution)/shard_map/while/body/eval_jaxpr/reduce_sum | solution.py:64
  123.1 24.6 %fusion.152 = (f32[8,784]{1,0:T(8,128)S(1)}, f32[8,784]{1,0:T(8,128)S(1)}) fusion(f32[784,256]{1,0:T(8,128)S(1)} %multiply_add_fusion.13, f32[8]{0:T(128)S(1)} %fusion.151, f32[256]{0:T(256)S(1)} %bitcast.427), kind=kLoop, calls=%fused_computation.132.clone.1 | loop fusion | flops 8015616 | bytes 854048 | tf_op jit(solution)/shard_map/while/body/eval_jaxpr/reduce_sum | solution.py:64
  148.9 24.6 %fusion.152 = (f32[8,784]{1,0:T(8,128)S(1)}, f32[8,784]{1,0:T(8,128)S(1)}) fusion(f32[784,256]{1,0:T(8,128)S(1)} %multiply_add_fusion.13, f32[8]{0:T(128)S(1)} %fusion.151, f32[256]{0:T(256)S(1)} %bitcast.427), kind=kLoop, calls=%fused_computation.132.clone.1 | loop fusion | flops 8015616 | bytes 854048 | tf_op jit(solution)/shard_map/while/body/eval_jaxpr/reduce_sum | solution.py:64
  174.6 24.6 %fusion.152 = (f32[8,784]{1,0:T(8,128)S(1)}, f32[8,784]{1,0:T(8,128)S(1)}) fusion(f32[784,256]{1,0:T(8,128)S(1)} %multiply_add_fusion.13, f32[8]{0:T(128)S(1)} %fusion.151, f32[256]{0:T(256)S(1)} %bitcast.427), kind=kLoop, calls=%fused_computation.132.clone.1 | loop fusion | flops 8015616 | bytes 854048 | tf_op jit(solution)/shard_map/while/body/eval_jaxpr/reduce_sum | solution.py:64
  200.4 24.6 %fusion.152 = (f32[8,784]{1,0:T(8,128)S(1)}, f32[8,784]{1,0:T(8,128)S(1)}) fusion(f32[784,256]{1,0:T(8,128)S(1)} %multiply_add_fusion.13, f32[8]{0:T(128)S(1)} %fusion.151, f32[256]{0:T(256)S(1)} %bitcast.427), kind=kLoop, calls=%fused_computation.132.clone.1 | loop fusion | flops 8015616 | bytes 854048 | tf_op jit(solution)/shard_map/while/body/eval_jaxpr/reduce_sum | solution.py:64
  226.2 24.6 %fusion.152 = (f32[8,784]{1,0:T(8,128)S(1)}, f32[8,784]{1,0:T(8,128)S(1)}) fusion(f32[784,256]{1,0:T(8,128)S(1)} %multiply_add_fusion.13, f32[8]{0:T(128)S(1)} %fusion.151, f32[256]{0:T(256)S(1)} %bitcast.427), kind=kLoop, calls=%fused_computation.132.clone.1 | loop fusion | flops 8015616 | bytes 854048 | tf_op jit(solution)/shard_map/while/body/eval_jaxpr/reduce_sum | solution.py:64
  251.9 154.8 %while.88 = (s32[]{:T(128)}, f32[6,2,8,784]{3,2,0,1:T(8,128)S(1)}, f32[1,256]{1,0:T(1,128)S(1)}, f32[6,8]{1,0:T(8,128)}, f32[256]{0:T(256)S(1)}, /*index=5*/f32[...) while((s32[]{:T(128)}, f32[6,2,8,784]{3,2,0,1:T(8,128)S(1)}, ...), condition=%wide.region_18.21_spmd.clone, body=%wide.region_15.20_spmd.clone.sunk | while | flops 9031682 | bytes 1784213 | solution.py:69
  253.2 24.6 %fusion.149 = (f32[8,784]{1,0:T(8,128)S(1)}, f32[8,784]{1,0:T(8,128)S(1)}) fusion(f32[784,256]{1,0:T(8,128)S(1)} %multiply_add_fusion.12, f32[8]{0:T(128)S(1)} %fusion.148, f32[256]{0:T(256)S(1)} %bitcast.428), kind=kLoop, calls=%fused_computation.121.clone.1 | loop fusion | flops 8015616 | bytes 854048 | tf_op jit(solution)/shard_map/while/body/eval_jaxpr/reduce_sum | solution.py:64
  279.0 24.6 %fusion.149 = (f32[8,784]{1,0:T(8,128)S(1)}, f32[8,784]{1,0:T(8,128)S(1)}) fusion(f32[784,256]{1,0:T(8,128)S(1)} %multiply_add_fusion.12, f32[8]{0:T(128)S(1)} %fusion.148, f32[256]{0:T(256)S(1)} %bitcast.428), kind=kLoop, calls=%fused_computation.121.clone.1 | loop fusion | flops 8015616 | bytes 854048 | tf_op jit(solution)/shard_map/while/body/eval_jaxpr/reduce_sum | solution.py:64
  304.8 24.6 %fusion.149 = (f32[8,784]{1,0:T(8,128)S(1)}, f32[8,784]{1,0:T(8,128)S(1)}) fusion(f32[784,256]{1,0:T(8,128)S(1)} %multiply_add_fusion.12, f32[8]{0:T(128)S(1)} %fusion.148, f32[256]{0:T(256)S(1)} %bitcast.428), kind=kLoop, calls=%fused_computation.121.clone.1 | loop fusion | flops 8015616 | bytes 854048 | tf_op jit(solution)/shard_map/while/body/eval_jaxpr/reduce_sum | solution.py:64
  330.5 24.6 %fusion.149 = (f32[8,784]{1,0:T(8,128)S(1)}, f32[8,784]{1,0:T(8,128)S(1)}) fusion(f32[784,256]{1,0:T(8,128)S(1)} %multiply_add_fusion.12, f32[8]{0:T(128)S(1)} %fusion.148, f32[256]{0:T(256)S(1)} %bitcast.428), kind=kLoop, calls=%fused_computation.121.clone.1 | loop fusion | flops 8015616 | bytes 854048 | tf_op jit(solution)/shard_map/while/body/eval_jaxpr/reduce_sum | solution.py:64
  356.3 24.6 %fusion.149 = (f32[8,784]{1,0:T(8,128)S(1)}, f32[8,784]{1,0:T(8,128)S(1)}) fusion(f32[784,256]{1,0:T(8,128)S(1)} %multiply_add_fusion.12, f32[8]{0:T(128)S(1)} %fusion.148, f32[256]{0:T(256)S(1)} %bitcast.428), kind=kLoop, calls=%fused_computation.121.clone.1 | loop fusion | flops 8015616 | bytes 854048 | tf_op jit(solution)/shard_map/while/body/eval_jaxpr/reduce_sum | solution.py:64
  382.1 24.6 %fusion.149 = (f32[8,784]{1,0:T(8,128)S(1)}, f32[8,784]{1,0:T(8,128)S(1)}) fusion(f32[784,256]{1,0:T(8,128)S(1)} %multiply_add_fusion.12, f32[8]{0:T(128)S(1)} %fusion.148, f32[256]{0:T(256)S(1)} %bitcast.428), kind=kLoop, calls=%fused_computation.121.clone.1 | loop fusion | flops 8015616 | bytes 854048 | tf_op jit(solution)/shard_map/while/body/eval_jaxpr/reduce_sum | solution.py:64
  418.8 21.4 %while.86 = (s32[]{:T(128)}, f32[8,3,8,128]{3,2,1,0:T(8,128)S(1)}, f32[8,4,8,128]{3,2,1,0:T(8,128)}, f32[8,4,8,512]{3,2,0,1:T(8,128)S(1)}, s32[]{:T(128)}, /*index=5*/s32[]{:T(128)}, s32[]{}, s32[]{}, s32[]{}) while((s32[]{:T(128)}, f32[8,3,8,128]{3,2,1,0:T(8,128)S(1)}, f32[8,4,8,128]{3,2,1,0:T(8,128)}, f32[8,4,8,512]{3,2,0,1:T(8,128)S(1)}, ...), condition=%wide.region_14.16_spmd, body=%wide.region_10.15_spmd.sunk | while | flops 8916997 | bytes 413849 | solution.py:140
  473.8 155.3 %while.91 = (s32[]{:T(128)}, f32[784,256]{1,0:T(8,128)S(1)}, f32[6,8]{1,0:T(8,128)}, f32[6,8,784]{2,1,0:T(8,128)}, f32[6,8,784]{2,1,0:T(8,128)S(1)}, /*index=5*/...) while((s32[]{:T(128)}, f32[784,256]{1,0:T(8,128)S(1)}, ...), condition=%wide.region_43.46_spmd.clone, body=%wide.region_41.45_spmd.clone.sunk | while | flops 10838019 | bytes 4980143 | solution.py:97
  475.7 23.8 %fusion.157 = f32[784,256]{1,0:T(8,128)S(1)} fusion(f32[8,784]{1,0:T(8,128)S(1)} %get-tuple-element.1153, f32[784,256]{1,0:T(8,128)S(1)} %multiply_add_fusion.15, f32[8,784]{1,0:T(8,128)S(1)} %get-tuple-element.1154, f32[8]{0:T(128)S(1)} %fusion.156), kind=kLoop, calls=%fused_computation.158.clone.1 | loop fusion | flops 9433088 | bytes 1655840 | tf_op jit(solution)/shard_map/while/body/eval_jaxpr/reduce_sum | solution.py:90
  501.6 23.8 %fusion.157 = f32[784,256]{1,0:T(8,128)S(1)} fusion(f32[8,784]{1,0:T(8,128)S(1)} %get-tuple-element.1153, f32[784,256]{1,0:T(8,128)S(1)} %multiply_add_fusion.15, f32[8,784]{1,0:T(8,128)S(1)} %get-tuple-element.1154, f32[8]{0:T(128)S(1)} %fusion.156), kind=kLoop, calls=%fused_computation.158.clone.1 | loop fusion | flops 9433088 | bytes 1655840 | tf_op jit(solution)/shard_map/while/body/eval_jaxpr/reduce_sum | solution.py:90
  527.5 23.8 %fusion.157 = f32[784,256]{1,0:T(8,128)S(1)} fusion(f32[8,784]{1,0:T(8,128)S(1)} %get-tuple-element.1153, f32[784,256]{1,0:T(8,128)S(1)} %multiply_add_fusion.15, f32[8,784]{1,0:T(8,128)S(1)} %get-tuple-element.1154, f32[8]{0:T(128)S(1)} %fusion.156), kind=kLoop, calls=%fused_computation.158.clone.1 | loop fusion | flops 9433088 | bytes 1655840 | tf_op jit(solution)/shard_map/while/body/eval_jaxpr/reduce_sum | solution.py:90
  553.3 23.8 %fusion.157 = f32[784,256]{1,0:T(8,128)S(1)} fusion(f32[8,784]{1,0:T(8,128)S(1)} %get-tuple-element.1153, f32[784,256]{1,0:T(8,128)S(1)} %multiply_add_fusion.15, f32[8,784]{1,0:T(8,128)S(1)} %get-tuple-element.1154, f32[8]{0:T(128)S(1)} %fusion.156), kind=kLoop, calls=%fused_computation.158.clone.1 | loop fusion | flops 9433088 | bytes 1655840 | tf_op jit(solution)/shard_map/while/body/eval_jaxpr/reduce_sum | solution.py:90
  579.2 23.8 %fusion.157 = f32[784,256]{1,0:T(8,128)S(1)} fusion(f32[8,784]{1,0:T(8,128)S(1)} %get-tuple-element.1153, f32[784,256]{1,0:T(8,128)S(1)} %multiply_add_fusion.15, f32[8,784]{1,0:T(8,128)S(1)} %get-tuple-element.1154, f32[8]{0:T(128)S(1)} %fusion.156), kind=kLoop, calls=%fused_computation.158.clone.1 | loop fusion | flops 9433088 | bytes 1655840 | tf_op jit(solution)/shard_map/while/body/eval_jaxpr/reduce_sum | solution.py:90
  605.1 23.8 %fusion.157 = f32[784,256]{1,0:T(8,128)S(1)} fusion(f32[8,784]{1,0:T(8,128)S(1)} %get-tuple-element.1153, f32[784,256]{1,0:T(8,128)S(1)} %multiply_add_fusion.15, f32[8,784]{1,0:T(8,128)S(1)} %get-tuple-element.1154, f32[8]{0:T(128)S(1)} %fusion.156), kind=kLoop, calls=%fused_computation.158.clone.1 | loop fusion | flops 9433088 | bytes 1655840 | tf_op jit(solution)/shard_map/while/body/eval_jaxpr/reduce_sum | solution.py:90
  629.3 150.9 %while.90 = (s32[]{:T(128)}, f32[784,256]{1,0:T(8,128)S(1)}, f32[6,8]{1,0:T(8,128)}, f32[6,8,784]{2,1,0:T(8,128)S(1)}, f32[6,8,784]{2,1,0:T(8,128)S(1)}, /*index...) while((s32[]{:T(128)}, f32[784,256]{1,0:T(8,128)S(1)}, ...), condition=%wide.region_24.27_spmd.clone, body=%wide.region_22.26_spmd.clone.sunk | while | flops 10838019 | bytes 4980143 | solution.py:97
  630.4 23.8 %fusion.155 = f32[784,256]{1,0:T(8,128)S(1)} fusion(f32[8,784]{1,0:T(8,128)S(1)} %get-tuple-element.1140, f32[784,256]{1,0:T(8,128)S(1)} %multiply_add_fusion.14, f32[8,784]{1,0:T(8,128)S(1)} %get-tuple-element.1141, f32[8]{0:T(128)S(1)} %fusion.154), kind=kLoop, calls=%fused_computation.145.clone.1 | loop fusion | flops 9433088 | bytes 1655840 | tf_op jit(solution)/shard_map/while/body/eval_jaxpr/reduce_sum | solution.py:90
  655.6 23.8 %fusion.155 = f32[784,256]{1,0:T(8,128)S(1)} fusion(f32[8,784]{1,0:T(8,128)S(1)} %get-tuple-element.1140, f32[784,256]{1,0:T(8,128)S(1)} %multiply_add_fusion.14, f32[8,784]{1,0:T(8,128)S(1)} %get-tuple-element.1141, f32[8]{0:T(128)S(1)} %fusion.154), kind=kLoop, calls=%fused_computation.145.clone.1 | loop fusion | flops 9433088 | bytes 1655840 | tf_op jit(solution)/shard_map/while/body/eval_jaxpr/reduce_sum | solution.py:90
  680.7 23.8 %fusion.155 = f32[784,256]{1,0:T(8,128)S(1)} fusion(f32[8,784]{1,0:T(8,128)S(1)} %get-tuple-element.1140, f32[784,256]{1,0:T(8,128)S(1)} %multiply_add_fusion.14, f32[8,784]{1,0:T(8,128)S(1)} %get-tuple-element.1141, f32[8]{0:T(128)S(1)} %fusion.154), kind=kLoop, calls=%fused_computation.145.clone.1 | loop fusion | flops 9433088 | bytes 1655840 | tf_op jit(solution)/shard_map/while/body/eval_jaxpr/reduce_sum | solution.py:90
  705.9 23.8 %fusion.155 = f32[784,256]{1,0:T(8,128)S(1)} fusion(f32[8,784]{1,0:T(8,128)S(1)} %get-tuple-element.1140, f32[784,256]{1,0:T(8,128)S(1)} %multiply_add_fusion.14, f32[8,784]{1,0:T(8,128)S(1)} %get-tuple-element.1141, f32[8]{0:T(128)S(1)} %fusion.154), kind=kLoop, calls=%fused_computation.145.clone.1 | loop fusion | flops 9433088 | bytes 1655840 | tf_op jit(solution)/shard_map/while/body/eval_jaxpr/reduce_sum | solution.py:90
  731.0 23.8 %fusion.155 = f32[784,256]{1,0:T(8,128)S(1)} fusion(f32[8,784]{1,0:T(8,128)S(1)} %get-tuple-element.1140, f32[784,256]{1,0:T(8,128)S(1)} %multiply_add_fusion.14, f32[8,784]{1,0:T(8,128)S(1)} %get-tuple-element.1141, f32[8]{0:T(128)S(1)} %fusion.154), kind=kLoop, calls=%fused_computation.145.clone.1 | loop fusion | flops 9433088 | bytes 1655840 | tf_op jit(solution)/shard_map/while/body/eval_jaxpr/reduce_sum | solution.py:90
  756.2 23.8 %fusion.155 = f32[784,256]{1,0:T(8,128)S(1)} fusion(f32[8,784]{1,0:T(8,128)S(1)} %get-tuple-element.1140, f32[784,256]{1,0:T(8,128)S(1)} %multiply_add_fusion.14, f32[8,784]{1,0:T(8,128)S(1)} %get-tuple-element.1141, f32[8]{0:T(128)S(1)} %fusion.154), kind=kLoop, calls=%fused_computation.145.clone.1 | loop fusion | flops 9433088 | bytes 1655840 | tf_op jit(solution)/shard_map/while/body/eval_jaxpr/reduce_sum | solution.py:90
  800.0 16.5 %while.87 = (s32[]{:T(128)}, f32[8,3,8,128]{3,2,1,0:T(8,128)S(1)}, f32[8,4,8,128]{3,2,1,0:T(8,128)S(1)}, f32[8,4,8,512]{3,2,0,1:T(8,128)S(1)}, s32[]{:T(128)}, /*index=5*/s32[]{:T(128)}, s32[]{}, s32[]{}, s32[]{}) while((s32[]{:T(128)}, f32[8,3,8,128]{3,2,1,0:T(8,128)S(1)}, f32[8,4,8,128]{3,2,1,0:T(8,128)S(1)}, ...), condition=%wide.region_33.36_spmd, body=%wide.region_29.35_spmd.sunk | while | flops 8916997 | bytes 413849 | solution.py:140
  (418 shorter events, 236.8 us)
Async XLA Ops:
  7.2 23.3 %copy-start.2 = (f32[1,3,8192]{2,0,1:T(1,128)S(1)}, f32[1,3,8192]{2,0,1:T(1,128)}, u32[]{:S(2)}) copy-start(f32[1,3,8192]{2,0,1:T(1,128)} %param.29) | copy-start | bytes 294916
  7.2 449.0 %all-reduce.4.cloned.1.call-start = ((), (), s32[]{:S(2)}) async-start(), calls=%async_computation | async-start | bytes 1376256 | tf_op jit(solution)/shard_map/psum | solution.py:174
  8.0 29.5 %collective-permute-start.2 = (f32[1,4096]{1,0:T(1,128)S(1)}, f32[1,4096]{1,0:T(1,128)S(1)}, u32[]{:S(2)}, u32[]{:S(2)}) collective-permute-start(f32[1,4096]{1,0:T(1,128)S(1)} %get-tuple-element.674), channel_id=1, source_target_pairs={{0,1},{1,2},{2,3},{4,5},{5,6},{6,7},{8,9},{9,10},{10,11},{12,13},{... | collective-permute-start | bytes 49160 | tf_op jit(solution)/shard_map/ppermute | solution.py:28
  12.9 24.6 %collective-permute-start.3 = (f32[1,4096]{1,0:T(1,128)S(1)}, f32[1,4096]{1,0:T(1,128)S(1)}, u32[]{:S(2)}, u32[]{:S(2)}) collective-permute-start(f32[1,4096]{1,0:T(1,128)S(1)} %get-tuple-element.673), channel_id=1, source_target_pairs={{1,0},{2,1},{3,2},{5,4},{6,5},{7,6},{9,8},{10,9},{11,10},{13,12},{... | collective-permute-start | bytes 49160 | tf_op jit(solution)/shard_map/ppermute | solution.py:30
  15.2 22.3 %collective-permute-start = (f32[3,4096]{1,0:T(4,128)S(1)}, f32[3,4096]{1,0:T(4,128)S(1)}, u32[]{:S(2)}, u32[]{:S(2)}) collective-permute-start(f32[3,4096]{1,0:T(4,128)S(1)} %get-tuple-element.671), channel_id=1, source_target_pairs={{0,1},{1,2},{2,3},{4,5},{5,6},{6,7},{8,9},{9,10},{10,11},{12,13},{... | collective-permute-start | bytes 147464 | tf_op jit(solution)/shard_map/ppermute | solution.py:28
  19.7 17.7 %collective-permute-start.1 = (f32[3,4096]{1,0:T(4,128)S(1)}, f32[3,4096]{1,0:T(4,128)S(1)}, u32[]{:S(2)}, u32[]{:S(2)}) collective-permute-start(f32[3,4096]{1,0:T(4,128)S(1)} %get-tuple-element.672), channel_id=1, source_target_pairs={{1,0},{2,1},{3,2},{5,4},{6,5},{7,6},{9,8},{10,9},{11,10},{13,12},{... | collective-permute-start | bytes 147464 | tf_op jit(solution)/shard_map/ppermute | solution.py:30
  31.2 6.2 copy-start.1
  39.1 16.6 %copy-start.3 = (f32[1,3,8192]{2,0,1:T(1,128)S(1)}, f32[1,3,8192]{2,0,1:T(1,128)}, u32[]{:S(2)}) copy-start(f32[1,3,8192]{2,0,1:T(1,128)} %param.30) | copy-start | bytes 294916
  56.1 6.7 collective-permute-start.4
  60.6 6.2 collective-permute-start.5
  90.1 5.7 copy-start.4
  90.1 5.7 copy-start.11
  90.1 6.1 copy-start.6
  406.7 11.9 %copy-start.7 = (f32[1,256]{1,0:T(1,128)}, f32[1,256]{1,0:T(1,128)S(1)}, u32[]{:S(2)}) copy-start(f32[1,256]{1,0:T(1,128)S(1)} %get-tuple-element.1447) | copy-start | bytes 3076
  406.8 11.5 %copy-start.10 = (pred[256]{0:T(512)(128)(4,1)S(1)}, pred[256]{0:T(512)(128)(4,1)}, u32[]{:S(2)}) copy-start(pred[256]{0:T(512)(128)(4,1)} %compare_and_fusion.2) | copy-start | bytes 772
  407.5 5.5 collective-permute-start.6
  411.0 6.2 collective-permute-start.7
  440.5 31.5 %copy-start.12 = (f32[48]{0:T(128)S(1)}, f32[48]{0:T(128)}, u32[]{:S(2)}) copy-start(f32[48]{0:T(128)} %param.36) | copy-start | bytes 580
  440.5 31.5 %copy-start.13 = (f32[48]{0:T(128)S(1)}, f32[48]{0:T(128)}, u32[]{:S(2)}) copy-start(f32[48]{0:T(128)} %param.37) | copy-start | bytes 580
  473.8 155.3 %copy-start = (f32[2,48,784]{2,1,0:T(8,128)S(1)}, f32[2,48,784]{2,1,0:T(8,128)}, u32[]{:S(2)}) copy-start(f32[2,48,784]{2,1,0:T(8,128)} %get-tuple-element.621) | copy-start | bytes 903172
  629.3 151.4 %copy-start.8 = (f32[1,256]{1,0:T(1,128)S(1)}, f32[1,256]{1,0:T(1,128)}, u32[]{:S(2)}) copy-start(f32[1,256]{1,0:T(1,128)} %copy-done.7) | copy-start | bytes 3076
  629.3 151.4 %copy-start.5 = (f32[256]{0:T(256)S(1)}, f32[256]{0:T(256)}, u32[]{:S(2)}) copy-start(f32[256]{0:T(256)} %broadcast_multiply_fusion.3) | copy-start | bytes 3076
  789.6 9.9 %copy-start.9 = (pred[256]{0:T(512)(128)(4,1)S(1)}, pred[256]{0:T(512)(128)(4,1)}, u32[]{:S(2)}) copy-start(pred[256]{0:T(512)(128)(4,1)} %compare_and_fusion) | copy-start | bytes 772
  789.7 4.3 collective-permute-start.8
  792.2 6.2 collective-permute-start.9
Sparse Core Ops, SparseCore 0:
  413.1 43.0 all-reduce.3
where the time goes:
time: 843 us; the launch traced here: 837 us
  other arithmetic  693 us (82%)
  local copies, waits for them, and re-layouts  59 us (7%)
  starting transfers between devices  26.6 us (3%)
  waiting for transfers between devices  25.9 us (3%)
  between operations  15.4 us (2%)
  blocking collectives  13.5 us (2%)
    reduce_sum x12, other arithmetic, one_block(): jnp.sum(weights * jnp.cos(phases), axis=-1)  296 us
    reduce_sum x12, other arithmetic, add_block(): jnp.sum(shell_block[:, None, None] * (block_imag[:, :, None] * jnp.cos(ph...  286 us
    reduce_sum x32, other arithmetic, pair_group(): jnp.sum(pair_weight * delta, axis=-1)  61.5 us
    ppermute x5, starting transfers between devices, extended_2(): lax.ppermute(tail, axis, [(i, (i + 1) % count) for i in range(ends)])  19.9 us
  transfers between devices with their start and end apart: 11, of which 5 were waited for; matrix products, arithmetic and copies ran while one was open for 5% of the time, Pallas kernels for 0%

commit v1 on v0

v1 whole, which is shorter than its diff:
```python
import functools
import math

import jax
import jax.numpy as jnp
import numpy as np
from jax import lax
from jax.experimental import pallas as pl
from jax.experimental.pallas import tpu as pltpu
from jax.sharding import PartitionSpec as P

M = 784
OUTER = 2
INNER = 2
TIME_STEP = 0.05
PAIR_STRENGTH = 0.2
HALF_INVERSE = 0.03125
LANES = 128
GROUP = 16
ROWS = 48
F32 = jnp.float32
BF16 = jnp.bfloat16
MESH = pl.DeviceIdType.MESH


def direction_table(shards):
    order = np.arange(M)
    height = 1.0 - (2.0 * order + 1.0) / M
    radius = np.sqrt(1.0 - height * height)
    azimuth = (order * 610 % 987) * (2.0 * math.pi / 987.0)
    rows = np.stack([radius * np.cos(azimuth), radius * np.sin(azimuth), height, np.ones(M)], axis=1)
    share = -(-M // shards)
    padded = -(-share // GROUP) * GROUP
    table = np.zeros((shards, padded, LANES), np.float32)
    for shard in range(shards):
        part = rows[shard * share : (shard + 1) * share]
        table[shard, : part.shape[0], :4] = part
    return table.reshape(shards, padded // GROUP, GROUP, LANES)


def dot(a, b, contract_a, contract_b, precision=None):
    return lax.dot_general(
        a, b, (((contract_a,), (contract_b,)), ((), ())), preferred_element_type=F32, precision=precision
    )


def split2(value):
    high = value.astype(BF16)
    return high, (value - high.astype(F32)).astype(BF16)


def split3(value):
    high = value.astype(BF16).astype(F32)
    rest = value - high
    middle = rest.astype(BF16).astype(F32)
    return high, middle, rest - middle


def sincos(angle):
    turns = jnp.floor(angle * (2.0 / math.pi) + 0.5)
    rest = angle - turns * 1.5703125
    rest = rest - turns * 4.837512969970703125e-4
    rest = rest - turns * 7.54978995489188216e-8
    square = rest * rest
    sine = rest + rest * square * (
        -1.6666654611e-1 + square * (8.3321608736e-3 - square * 1.9515295891e-4)
    )
    cosine = 1.0 - 0.5 * square + square * square * (
        4.166664568298827e-2 + square * (-1.388731625493765e-3 + square * 2.443315711809948e-5)
    )
    quadrant = turns.astype(jnp.int32)
    odd = (quadrant & 1) == 1
    first = jnp.where(odd, sine, cosine)
    second = jnp.where(odd, cosine, sine)
    first = jnp.where(((quadrant + 1) & 2) == 2, -first, first)
    second = jnp.where((quadrant & 2) == 2, -second, second)
    return first, second


def kernel(
    dims,
    fourth_ref,
    pos_ref,
    vel_ref,
    strength_ref,
    mass_ref,
    solute_ref,
    weight_ref,
    shell_ref,
    table_ref,
    pos_out,
    vel_out,
    states,
    halo_left,
    halo_right,
    speed,
    factor,
    near,
    own,
    points,
    level_sp,
    level_rep,
    kick_out,
    kick_in,
    e_high,
    e_low,
    f_high,
    f_low,
    amp_real,
    amp_imag,
    level,
    gains,
    kick_sum,
    halo_send,
    halo_recv,
    point_send,
    point_recv,
    sp_send,
    sp_recv,
    rep_send,
    rep_recv,
    kick_send,
    kick_recv,
):
    count, replicas, blocks, slots, coarse, fine, groups = dims
    rim = blocks // 2
    me = lax.axis_index("sp")
    rep = lax.axis_index("rep")
    q_step = 3.0 / (coarse * fine)
    all_slots = count * slots
    e_half = coarse * GROUP
    f_half = fine * GROUP

    def sp_peer(distance):
        return (rep, lax.rem(me + distance, count))

    def rep_peer(distance):
        return (lax.rem(rep + distance, replicas), me)

    barrier = pltpu.get_barrier_semaphore()
    for distance in range(1, count):
        pl.semaphore_signal(barrier, inc=1, device_id=sp_peer(distance), device_id_type=MESH)
    for distance in range(1, replicas):
        pl.semaphore_signal(barrier, inc=1, device_id=rep_peer(distance), device_id_type=MESH)

    for block in range(blocks):
        span = slice(block * LANES, (block + 1) * LANES)
        strength = strength_ref[:, span]
        states[0, block] = jnp.concatenate(
            [pos_ref[0, :, span], jnp.log(strength), jnp.ones((1, LANES), F32), jnp.zeros((3, LANES), F32)], axis=0
        )
        speed[block] = jnp.concatenate([vel_ref[0, :, span], jnp.zeros((5, LANES), F32)], axis=0)
        coupling = TIME_STEP * PAIR_STRENGTH / math.sqrt(4 * LANES)
        push = jnp.broadcast_to(coupling * strength * mass_ref[:, span], (3, LANES))
        factor[block] = jnp.concatenate([push, jnp.zeros((5, LANES), F32)], axis=0)

    @pl.when(me == 0)
    def _():
        halo_left[...] = jnp.zeros_like(halo_left)

    @pl.when(me == count - 1)
    def _():
        halo_right[...] = jnp.zeros_like(halo_right)

    pl.semaphore_wait(barrier, count - 1 + replicas - 1)

    def halo_copies(step):
        to_right = pltpu.make_async_remote_copy(
            src_ref=states.at[step, pl.ds(blocks - rim, rim)],
            dst_ref=halo_left.at[step],
            send_sem=halo_send.at[step, 0],
            recv_sem=halo_recv.at[step, 0],
            device_id=sp_peer(1),
            device_id_type=MESH,
        )
        to_left = pltpu.make_async_remote_copy(
            src_ref=states.at[step, pl.ds(0, rim)],
            dst_ref=halo_right.at[step],
            send_sem=halo_send.at[step, 1],
            recv_sem=halo_recv.at[step, 1],
            device_id=sp_peer(count - 1),
            device_id_type=MESH,
        )
        return to_right, to_left

    def start_halo(step):
        to_right, to_left = halo_copies(step)
        pl.when(me < count - 1)(to_right.start)
        pl.when(me > 0)(to_left.start)

    def finish_halo(step):
        to_right, to_left = halo_copies(step)
        pl.when(me < count - 1)(to_right.wait_send)
        pl.when(me > 0)(to_left.wait_send)
        pl.when(me > 0)(to_right.wait_recv)
        pl.when(me < count - 1)(to_left.wait_recv)

    def group_copies(source, target, send, recv, outer, peer, size):
        return [
            pltpu.make_async_remote_copy(
                src_ref=source(distance),
                dst_ref=target,
                send_sem=send.at[outer, distance],
                recv_sem=recv.at[outer, distance],
                device_id=peer(distance),
                device_id_type=MESH,
            )
            for distance in range(1, size)
        ]

    def start_all(copies):
        for copy in copies:
            copy.start()

    def wait_all(copies):
        for copy in copies:
            copy.wait()

    row = lax.broadcasted_iota(jnp.int32, (1, 8, LANES), 1)

    def block_features(state):
        radius = HALF_INVERSE * jnp.sum(jnp.where(row < 3, state * state, 0.0), axis=1, keepdims=True)
        return radius, jnp.where(row == 3, state - radius, state)

    def near_features(target, state):
        radius, value = block_features(state)
        high, middle, low = split3(value)
        near[pl.ds(target, state.shape[0])] = jnp.concatenate(
            [high, middle, high, middle, low, high], axis=1
        ).astype(BF16)

    def own_features(index, state):
        radius, value = block_features(state)
        near_side = jnp.where(row < 3, state * (2.0 * HALF_INVERSE), 0.0)
        value = near_side + jnp.where(row == 3, 1.0, 0.0) - jnp.where(row == 4, radius, 0.0)
        high, middle, low = split3(value)
        rows = jnp.concatenate([high, high, middle, middle, high, low], axis=1)
        for k in range(state.shape[0]):
            own[index + k] = rows[k].T.astype(BF16)

    chunk = 4

    def build_own(step):
        @pl.loop(0, blocks // chunk)
        def _(i):
            state = states[step, pl.ds(i * chunk, chunk)]
            near_features(rim + i * chunk, state)
            own_features(i * chunk, state)

    def build_halo(step):
        @pl.loop(0, rim // chunk)
        def _(i):
            near_features(i * chunk, halo_left[step, pl.ds(i * chunk, chunk)])
            near_features(rim + blocks + i * chunk, halo_right[step, pl.ds(i * chunk, chunk)])

    def pair_step(step):
        def one(block):
            sides = [near[block], near[block + rim], near[block + 2 * rim], near[fourth_ref[step, block]]]
            features = jnp.concatenate(sides, axis=1)
            weight = jnp.exp(dot(own[block], features, 1, 0)).astype(BF16)
            sums = dot(features[:16], weight, 1, 1)
            sums = sums[:8] + sums[8:]
            state = states[step, block]
            velocity = speed[block] + factor[block] * (state * sums[4:5] - sums)
            speed[block] = velocity
            states[step + 1, block] = state + TIME_STEP * velocity

        unroll = 4

        @pl.loop(0, blocks // unroll)
        def _(i):
            for k in range(unroll):
                one(i * unroll + k)

    slot_index = solute_ref[...]
    pick_block = (lax.broadcasted_iota(jnp.int32, (blocks, slots), 0) == slot_index // LANES)
    pick_lane = (lax.broadcasted_iota(jnp.int32, (LANES, slots), 0) == slot_index % LANES)
    block_hot = pick_block.astype(F32)
    lane_hot = pick_lane.astype(F32)

    def gather_points(step, outer):
        found = []
        for axis in range(3):
            plane = states[step, :, axis, :].T
            parts = split3(plane)
            spread = sum(dot(part.astype(BF16), block_hot.astype(BF16), 1, 0) for part in parts)
            found.append(jnp.sum(spread * lane_hot, axis=0, keepdims=True))
        points[outer, me] = jnp.concatenate(
            found + [weight_ref[...], jnp.zeros((4, slots), F32)], axis=0
        )

    def amplitudes(outer):
        level[...] = jnp.zeros_like(level)
        width = slots

        @pl.loop(0, groups)
        def _(g):
            directions = table_ref[me, g]
            for part in range(count):
                span = slice(part * width, (part + 1) * width)
                spot = points[outer, part]
                project = (
                    directions[:, 0:1] * spot[0:1] + directions[:, 1:2] * spot[1:2] + directions[:, 2:3] * spot[2:3]
                )

                def put(high_ref, low_ref, at, value):
                    high, low = split2(value)
                    high_ref[g, at : at + GROUP, span] = high
                    low_ref[g, at : at + GROUP, span] = low

                step_cos, step_sin = sincos(q_step * project)
                twice = 2.0 * step_cos
                old = (jnp.ones_like(project), jnp.zeros_like(project))
                new = (step_cos, step_sin)
                for b in range(fine):
                    put(f_high, f_low, b * GROUP, old[0])
                    put(f_high, f_low, f_half + b * GROUP, old[1])
                    old, new = new, (twice * new[0] - old[0], twice * new[1] - old[1])
                jump_cos, jump_sin = old
                real, imag = sincos(project)
                scale = spot[3:4] * directions[:, 3:4]
                real, imag = real * scale, imag * scale
                for a in range(coarse):
                    put(e_high, e_low, a * GROUP, real)
                    put(e_high, e_low, e_half + a * GROUP, imag)
                    real, imag = real * jump_cos - imag * jump_sin, real * jump_sin + imag * jump_cos
            total = (
                dot(e_high[g], f_high[g], 1, 1) + dot(e_high[g], f_low[g], 1, 1) + dot(e_low[g], f_high[g], 1, 1)
            )
            real = total[:e_half, :f_half] - total[e_half:, f_half:]
            imag = total[e_half:, :f_half] + total[:e_half, f_half:]
            amp_real[g] = real
            amp_imag[g] = imag
            level[...] += real * real + imag * imag

        diagonal = diagonal_mask()
        kept = jnp.where(diagonal, level[...], 0.0)
        sums = [jnp.sum(kept[a * GROUP : (a + 1) * GROUP], axis=0, keepdims=True) for a in range(coarse)]
        level_sp[outer, me] = jnp.concatenate(sums + [jnp.zeros((8 - coarse, f_half), F32)], axis=0)

    def diagonal_mask():
        rows = lax.broadcasted_iota(jnp.int32, (e_half, f_half), 0)
        columns = lax.broadcasted_iota(jnp.int32, (e_half, f_half), 1)
        return rows % GROUP == columns % GROUP

    def shell_gains(outer):
        total = level_rep[outer, 0]
        for k in range(1, replicas):
            total = total + level_rep[outer, k]
        rows = lax.broadcasted_iota(jnp.int32, (f_half, f_half), 0)
        columns = lax.broadcasted_iota(jnp.int32, (f_half, f_half), 1)
        same = (rows // GROUP == columns // GROUP).astype(F32)
        shells = dot(total, same, 1, 0, lax.Precision.HIGHEST) / (all_slots * M * replicas)
        coefficient = shell_ref[2] * shell_ref[1] * (shells - shell_ref[0])
        wide = jnp.concatenate(
            [jnp.broadcast_to(coefficient[a : a + 1], (GROUP, f_half)) for a in range(coarse)], axis=0
        )
        gains[...] = jnp.where(diagonal_mask(), wide, 0.0)

    def kicks(outer):
        kick_sum[...] = jnp.zeros_like(kick_sum)

        @pl.loop(0, groups)
        def _(g):
            real = gains[...] * amp_real[g]
            imag = gains[...] * amp_imag[g]
            mixed = jnp.concatenate(
                [jnp.concatenate([real, imag], axis=1), jnp.concatenate([imag, -real], axis=1)], axis=0
            )
            high, low = split2(mixed)
            directions = table_ref[me, g]
            for part in range(count):
                span = slice(part * slots, (part + 1) * slots)
                shells_high = f_high[g, :, span]
                turned = (
                    dot(high, shells_high, 1, 0) + dot(low, shells_high, 1, 0) + dot(high, f_low[g, :, span], 1, 0)
                )
                waves = e_high[g, :, span].astype(F32) + e_low[g, :, span].astype(F32)
                force = jnp.zeros((GROUP, slots), F32)
                for a in range(coarse):
                    here = slice(a * GROUP, (a + 1) * GROUP)
                    there = slice(e_half + a * GROUP, e_half + (a + 1) * GROUP)
                    force = force + waves[here] * turned[there] - waves[there] * turned[here]
                for axis in range(3):
                    kick_sum[axis, :, span] += directions[:, axis : axis + 1] * force

        for part in range(count):
            span = slice(part * slots, (part + 1) * slots)
            sums = [-jnp.sum(kick_sum[axis, :, span], axis=0, keepdims=True) for axis in range(3)]
            kick_out[outer, part] = jnp.concatenate(sums + [jnp.zeros((5, slots), F32)], axis=0)

    def apply_kicks(outer):
        total = kick_in[outer, 0]
        for k in range(1, count):
            total = total + kick_in[outer, k]
        lanes = lane_hot.astype(BF16)
        for axis in range(3):
            parts = split3(total[axis : axis + 1] * block_hot)
            spread = sum(dot(part.astype(BF16), lanes, 1, 1) for part in parts)
            for block in range(blocks):
                mass = mass_ref[:, block * LANES : (block + 1) * LANES]
                speed[block, axis : axis + 1] += (INNER * TIME_STEP) * mass * spread[block : block + 1]

    start_halo(0)
    for outer in range(OUTER):
        first = outer * INNER
        gather_points(first, outer)
        point_copies = group_copies(
            lambda d: points.at[outer, me], points.at[outer, me], point_send, point_recv, outer, sp_peer, count
        )
        start_all(point_copies)
        build_own(first)
        wait_all(point_copies)
        amplitudes(outer)
        sp_copies = group_copies(
            lambda d: level_sp.at[outer, me], level_sp.at[outer, me], sp_send, sp_recv, outer, sp_peer, count
        )
        start_all(sp_copies)
        finish_halo(first)
        build_halo(first)
        wait_all(sp_copies)
        total = level_sp[outer, 0]
        for k in range(1, count):
            total = total + level_sp[outer, k]
        level_rep[outer, rep] = total
        rep_copies = group_copies(
            lambda d: level_rep.at[outer, rep], level_rep.at[outer, rep], rep_send, rep_recv, outer, rep_peer, replicas
        )
        start_all(rep_copies)
        pair_step(first)
        for inner in range(1, INNER):
            step = first + inner
            start_halo(step)
            build_own(step)
            if inner == 1:
                wait_all(rep_copies)
                shell_gains(outer)
                kicks(outer)
                kick_in[outer, me] = kick_out[outer, me]
                kick_copies = group_copies(
                    lambda d: kick_out.at[outer, lax.rem(me + d, count)],
                    kick_in.at[outer, me],
                    kick_send,
                    kick_recv,
                    outer,
                    sp_peer,
                    count,
                )
                start_all(kick_copies)
            finish_halo(step)
            build_halo(step)
            pair_step(step)
        if outer + 1 < OUTER:
            start_halo(first + INNER)
        wait_all(kick_copies)
        apply_kicks(outer)

    for block in range(blocks):
        span = slice(block * LANES, (block + 1) * LANES)
        pos_out[0, :, span] = states[OUTER * INNER, block, 0:3]
        vel_out[0, :, span] = speed[block, 0:3]


def solution(mesh):
    count, replicas = mesh.shape["sp"], mesh.shape["rep"]
    table = direction_table(count)
    groups = table.shape[1]
    steps = OUTER * INNER

    def shards(
        positions, velocities, strength, inv_mass, tile_lists, solute_index, scatter_weight, intensity_exp, precision
    ):
        atoms = positions.shape[2]
        blocks = atoms // LANES
        rim = blocks // 2
        slots = solute_index.shape[1]
        shells = intensity_exp.shape[0]
        fine = LANES // GROUP
        coarse = shells // fine
        order = jnp.arange(blocks, dtype=jnp.int32)
        fourth = jnp.sum(tile_lists[0], axis=-1) - 3 * (order + rim)[None, :]
        q = 1.0 + 3.0 * jnp.arange(shells, dtype=F32) / shells
        gain = 2.0 * precision * q / (M * math.sqrt(count * slots))
        rows = jnp.stack([intensity_exp, gain, jnp.ones_like(q)]).reshape(3, coarse, fine)
        rows = jnp.pad(jnp.repeat(rows, GROUP, axis=2), ((0, 0), (0, 8 - coarse), (0, 0)))
        e_rows, f_rows, wide = 2 * coarse * GROUP, 2 * fine * GROUP, count * slots
        vmem = pl.BlockSpec(memory_space=pltpu.VMEM)
        dma = pltpu.SemaphoreType.DMA
        return pl.pallas_call(
            functools.partial(kernel, (count, replicas, blocks, slots, coarse, fine, groups)),
            out_shape=(
                jax.ShapeDtypeStruct(positions.shape, F32),
                jax.ShapeDtypeStruct(velocities.shape, F32),
            ),
            in_specs=[pl.BlockSpec(memory_space=pltpu.SMEM)] + [vmem] * 8,
            out_specs=(vmem, vmem),
            scratch_shapes=[
                pltpu.VMEM((steps + 1, blocks, 8, LANES), F32),
                pltpu.VMEM((steps, rim, 8, LANES), F32),
                pltpu.VMEM((steps, rim, 8, LANES), F32),
                pltpu.VMEM((blocks, 8, LANES), F32),
                pltpu.VMEM((blocks, 8, LANES), F32),
                pltpu.VMEM((2 * blocks, ROWS, LANES), BF16),
                pltpu.VMEM((blocks, LANES, ROWS), BF16),
                pltpu.VMEM((OUTER, count, 8, slots), F32),
                pltpu.VMEM((OUTER, count, 8, LANES), F32),
                pltpu.VMEM((OUTER, replicas, 8, LANES), F32),
                pltpu.VMEM((OUTER, count, 8, slots), F32),
                pltpu.VMEM((OUTER, count, 8, slots), F32),
                pltpu.VMEM((groups, e_rows, wide), BF16),
                pltpu.VMEM((groups, e_rows, wide), BF16),
                pltpu.VMEM((groups, f_rows, wide), BF16),
                pltpu.VMEM((groups, f_rows, wide), BF16),
                pltpu.VMEM((groups, e_rows // 2, f_rows // 2), F32),
                pltpu.VMEM((groups, e_rows // 2, f_rows // 2), F32),
                pltpu.VMEM((e_rows // 2, f_rows // 2), F32),
                pltpu.VMEM((e_rows // 2, f_rows // 2), F32),
                pltpu.VMEM((3, GROUP, wide), F32),
                dma((steps, 2)),
                dma((steps, 2)),
                dma((OUTER, count)),
                dma((OUTER, count)),
                dma((OUTER, count)),
                dma((OUTER, count)),
                dma((OUTER, replicas)),
                dma((OUTER, replicas)),
                dma((OUTER, count)),
                dma((OUTER, count)),
            ],
            compiler_params=pltpu.CompilerParams(
                collective_id=0, has_side_effects=True, vmem_limit_bytes=58 * 1024 * 1024
            ),
            cost_estimate=pl.CostEstimate(flops=40_000_000_000, bytes_accessed=4_000_000, transcendentals=20_000_000),
        )(fourth, positions, velocities, strength, inv_mass, solute_index, scatter_weight, rows, jnp.asarray(table))

    in_specs = (
        P("rep", None, "sp"),
        P("rep", None, "sp"),
        P("rep", "sp"),
        P("rep", "sp"),
        P("rep", None, "sp", None),
        P("rep", "sp"),
        P("rep", "sp"),
        P(),
        P(),
    )
    out_specs = (P("rep", None, "sp"), P("rep", None, "sp"))
    return jax.shard_map(shards, mesh=mesh, in_specs=in_specs, out_specs=out_specs, check_vma=False)
```

time: 843 us -> 114 us (0.14)
  other arithmetic: 693 us -> 1.39 us
  Pallas kernels: 0 us -> 105 us
  local copies, waits for them, and re-layouts: 59 us -> 6.36 us
  starting transfers between devices: 26.6 us -> 0 us
  waiting for transfers between devices: 25.9 us -> 0 us
  between operations: 15.4 us -> 0.67 us
  blocking collectives: 13.5 us -> 0 us
    reduce_sum x59 -> x1, other arithmetic: 645 us -> 0.71 us  [shards(): fourth = jnp.sum(tile_lists[0], axis=-1) - 3 * (order + rim)[None, :]]
    pallas_call x0 -> x1, Pallas kernels: none -> 105 us  [shards(): pl.pallas_call(functools.partial(kernel, (count, replicas, blocks, slots,...]
    ppermute x10 -> x0, starting transfers between devices: 26.6 us -> none  [the longest x5 19.9 us: extended_2(): lax.ppermute(tail, axis, [(i, (i + 1) % count) for i in range(ends)])]
    mul x70 -> x0, local copies, waits for them, and re-layouts: 21.9 us -> none  [the longest x12 8.37 us: one_block(): phases = shell_block[:, None, None] * project[None]]
    mul x41 -> x1, other arithmetic: 15.6 us -> 0.01 us  [shards(): fourth = jnp.sum(tile_lists[0], axis=-1) - 3 * (order + rim)[None, :]]
    psum x1 -> x0, blocking collectives: 13.5 us -> none  [shards(): intensity = lax.psum(shell_intensity(amplitude), 'rep') / replica_count]
    psum x1 -> x0, waiting for transfers between devices: 13 us -> none  [shards(): amplitude = lax.psum(partial_value, 'sp')]
    ppermute x10 -> x0, waiting for transfers between devices: 12.9 us -> none  [the longest x5 12.4 us: extended_2(): lax.ppermute(head, axis, [((i + 1) % count, i) for i in range(ends)])]
  transfers between devices with their start and end apart: 11 -> 0, of which waited for: 5 -> 0; matrix products, arithmetic and copies ran while one was open for 5% -> 0% of each run, Pallas kernels for 0% -> 0%
where the time goes in v1:
time: 114 us; the launch traced here: 113 us
  Pallas kernels  105 us (92%)
  local copies, waits for them, and re-layouts  6.36 us (6%)
  other arithmetic  1.39 us (1%)
    pallas_call x1, Pallas kernels, shards(): pl.pallas_call(functools.partial(kernel, (count, replicas, blocks, slots,...  105 us
    unnamed x12, local copies, waits for them, and re-layouts  2.93 us
    pallas_call x2, local copies, waits for them, and re-layouts, shards(): pl.pallas_call(functools.partial(kernel, (count, replicas, blocks, slots,...  2.42 us

profile of v1, /device:TPU:0, one launch (start us, length us, event | category | flops | bytes accessed | tf_op | source)
XLA Modules:
  0.0 113.4 jit_solution(4512449038800581151)
XLA Ops:
  0.6 0.0 copy-start.4
  0.6 0.6 copy-done.4
  1.3 0.1 pad.7.clone
  1.4 0.7 reduce_sum.9
  2.1 0.6 broadcast_subtract_fusion.fourth_ref
  2.7 0.0 copy-start.3
  2.7 0.1 stack.10
  2.8 0.6 copy-done.3
  3.3 0.1 stack.9
  3.4 0.1 maximum_maximum_fusion
  3.5 0.0 copy-start.1
  3.5 0.1 broadcast_in_dim.4
  3.6 0.1 reshape.19
  3.7 0.6 pad.4.shell_ref
  4.3 0.1 copy-done.1
  4.4 0.0 copy-start.2
  4.4 0.7 copy.16.pos_ref
  5.1 0.2 copy-done.2
  5.3 0.7 copy.17.vel_ref
  6.0 105.0 %shard_map.113 = (f32[1,3,8192]{2,1,0:T(4,128)}, f32[1,3,8192]{2,1,0:T(4,128)}) custom-call(s32[4,64]{1,0:T(4,128)} %broadcast_subtract_fusion.fourth_ref, f32[1,3,8192]{2,1,0:T(4,128)} %copy.16.pos_ref, f32[1,3,8192]{2,1,0:T(4,128)} %copy.17.vel_ref, f32[1,8192]{1,0:T(1,128)} %strength_ref.1, f32[1,8192]{1,0:T(1,128)} %mass_ref.1, s32[1,256]{1,0:T(1,128)} %solute_ref.1, ...), custom_call_target="tpu_custom_call" | custom-call | flops 40000000000 | bytes 4000000 | tf_op jit(solution)/shard_map/pallas_call | solution.py:489
  110.9 0.0 copy-start
  111.0 1.7 %copy.18 = f32[1,3,8192]{2,0,1:T(1,128)} copy(f32[1,3,8192]{2,1,0:T(4,128)} %get-tuple-element.4) | data formatting | bytes 196608 | tf_op jit(solution)/shard_map/pallas_call | solution.py:489
  112.6 0.0 copy-done
  112.6 0.7 copy.19
  (2 shorter events, 0.0 us)
Async XLA Ops:
  0.6 0.7 copy-start.4
  2.7 0.7 copy-start.3
  3.5 0.9 copy-start.1
  4.4 0.9 copy-start.2
  110.9 1.7 %copy-start = (f32[1,3,8192]{2,1,0:T(4,128)S(1)}, f32[1,3,8192]{2,1,0:T(4,128)}, u32[]{:S(2)}) copy-start(f32[1,3,8192]{2,1,0:T(4,128)} %get-tuple-element.5) | copy-start | bytes 294916

commit v2 on v1

--- a/solution.py
+++ b/solution.py
@@ -79,14 +79,15 @@
 
 def kernel(
     dims,
-    fourth_ref,
+    tile_ref,
     pos_ref,
     vel_ref,
     strength_ref,
     mass_ref,
     solute_ref,
     weight_ref,
-    shell_ref,
+    target_ref,
+    precision_ref,
     table_ref,
     pos_out,
     vel_out,
@@ -95,8 +96,10 @@
     halo_right,
     speed,
     factor,
-    near,
-    own,
+    near_even,
+    near_odd,
+    own_even,
+    own_odd,
     points,
     level_sp,
     level_rep,
@@ -143,16 +146,17 @@
     for distance in range(1, replicas):
         pl.semaphore_signal(barrier, inc=1, device_id=rep_peer(distance), device_id_type=MESH)
 
-    for block in range(blocks):
-        span = slice(block * LANES, (block + 1) * LANES)
-        strength = strength_ref[:, span]
-        states[0, block] = jnp.concatenate(
-            [pos_ref[0, :, span], jnp.log(strength), jnp.ones((1, LANES), F32), jnp.zeros((3, LANES), F32)], axis=0
-        )
-        speed[block] = jnp.concatenate([vel_ref[0, :, span], jnp.zeros((5, LANES), F32)], axis=0)
-        coupling = TIME_STEP * PAIR_STRENGTH / math.sqrt(4 * LANES)
-        push = jnp.broadcast_to(coupling * strength * mass_ref[:, span], (3, LANES))
-        factor[block] = jnp.concatenate([push, jnp.zeros((5, LANES), F32)], axis=0)
+    row = lax.broadcasted_iota(jnp.int32, (1, 8, LANES), 1)
+    strength = strength_ref[...]
+    push = (TIME_STEP * PAIR_STRENGTH / math.sqrt(4 * LANES)) * strength * mass_ref[...]
+    states[0] = jnp.broadcast_to(jnp.where(row == 4, 1.0, 0.0), (blocks, 8, LANES))
+    speed[...] = jnp.zeros_like(speed)
+    factor[...] = jnp.zeros_like(factor)
+    states[0, :, 3, :] = jnp.log(strength)
+    for axis in range(3):
+        states[0, :, axis, :] = pos_ref[axis]
+        speed[:, axis, :] = vel_ref[axis]
+        factor[:, axis, :] = push
 
     @pl.when(me == 0)
     def _():
@@ -216,20 +220,18 @@
         for copy in copies:
             copy.wait()
 
-    row = lax.broadcasted_iota(jnp.int32, (1, 8, LANES), 1)
-
     def block_features(state):
         radius = HALF_INVERSE * jnp.sum(jnp.where(row < 3, state * state, 0.0), axis=1, keepdims=True)
         return radius, jnp.where(row == 3, state - radius, state)
 
-    def near_features(target, state):
+    def near_features(near, target, state):
         radius, value = block_features(state)
         high, middle, low = split3(value)
         near[pl.ds(target, state.shape[0])] = jnp.concatenate(
             [high, middle, high, middle, low, high], axis=1
         ).astype(BF16)
 
-    def own_features(index, state):
+    def own_features(own, index, state):
         radius, value = block_features(state)
         near_side = jnp.where(row < 3, state * (2.0 * HALF_INVERSE), 0.0)
         value = near_side + jnp.where(row == 3, 1.0, 0.0) - jnp.where(row == 4, radius, 0.0)
@@ -238,34 +240,47 @@
         for k in range(state.shape[0]):
             own[index + k] = rows[k].T.astype(BF16)
 
-    chunk = 4
+    chunk = 8
+    nears, owns = (near_even, near_odd), (own_even, own_odd)
 
     def build_own(step):
         @pl.loop(0, blocks // chunk)
         def _(i):
             state = states[step, pl.ds(i * chunk, chunk)]
-            near_features(rim + i * chunk, state)
-            own_features(i * chunk, state)
+            near_features(nears[step % 2], rim + i * chunk, state)
+            own_features(owns[step % 2], i * chunk, state)
 
     def build_halo(step):
         @pl.loop(0, rim // chunk)
         def _(i):
-            near_features(i * chunk, halo_left[step, pl.ds(i * chunk, chunk)])
-            near_features(rim + blocks + i * chunk, halo_right[step, pl.ds(i * chunk, chunk)])
+            near_features(nears[step % 2], i * chunk, halo_left[step, pl.ds(i * chunk, chunk)])
+            near_features(nears[step % 2], rim + blocks + i * chunk, halo_right[step, pl.ds(i * chunk, chunk)])
 
     def pair_step(step):
+        near, own = nears[step % 2], owns[step % 2]
+        near_next, own_next = nears[(step + 1) % 2], owns[(step + 1) % 2]
+
         def one(block):
-            sides = [near[block], near[block + rim], near[block + 2 * rim], near[fourth_ref[step, block]]]
-            features = jnp.concatenate(sides, axis=1)
-            weight = jnp.exp(dot(own[block], features, 1, 0)).astype(BF16)
-            sums = dot(features[:16], weight, 1, 1)
+            fourth = tile_ref[step, 0, block] + tile_ref[step, 1, block] + tile_ref[step, 2, block]
+            fourth = fourth + tile_ref[step, 3, block] - 3 * (block + rim)
+            fourth = jnp.clip(fourth, 0, 2 * blocks - 1)
+            mine = own[block]
+            sums = jnp.zeros((16, LANES), F32)
+            for pair in ((block, block + rim), (block + 2 * rim, fourth)):
+                features = jnp.concatenate([near[pair[0]], near[pair[1]]], axis=1)
+                weight = jnp.exp(dot(mine, features, 1, 0)).astype(BF16)
+                sums = sums + dot(features[:16], weight, 1, 1)
             sums = sums[:8] + sums[8:]
             state = states[step, block]
             velocity = speed[block] + factor[block] * (state * sums[4:5] - sums)
             speed[block] = velocity
-            states[step + 1, block] = state + TIME_STEP * velocity
-
-        unroll = 4
+            state = state + TIME_STEP * velocity
+            states[step + 1, block] = state
+            if step + 1 < OUTER * INNER:
+                near_features(near_next, rim + block, state[None])
+                own_features(own_next, block, state[None])
+
+        unroll = 8 if blocks % 8 == 0 else 1
 
         @pl.loop(0, blocks // unroll)
         def _(i):
@@ -296,6 +311,7 @@
         @pl.loop(0, groups)
         def _(g):
             directions = table_ref[me, g]
+            total = jnp.zeros((2 * e_half, 2 * f_half), F32)
             for part in range(count):
                 span = slice(part * width, (part + 1) * width)
                 spot = points[outer, part]
@@ -317,16 +333,20 @@
                     put(f_high, f_low, f_half + b * GROUP, old[1])
                     old, new = new, (twice * new[0] - old[0], twice * new[1] - old[1])
                 jump_cos, jump_sin = old
-                real, imag = sincos(project)
+                if 3 * 2 * fine == coarse * fine:
+                    real, imag = jump_cos * jump_cos - jump_sin * jump_sin, 2.0 * jump_cos * jump_sin
+                else:
+                    real, imag = sincos(project)
                 scale = spot[3:4] * directions[:, 3:4]
                 real, imag = real * scale, imag * scale
                 for a in range(coarse):
                     put(e_high, e_low, a * GROUP, real)
                     put(e_high, e_low, e_half + a * GROUP, imag)
                     real, imag = real * jump_cos - imag * jump_sin, real * jump_sin + imag * jump_cos
-            total = (
-                dot(e_high[g], f_high[g], 1, 1) + dot(e_high[g], f_low[g], 1, 1) + dot(e_low[g], f_high[g], 1, 1)
-            )
+                waves, bands = e_high[g, :, span], f_high[g, :, span]
+                waves = jnp.concatenate([waves, waves, e_low[g, :, span]], axis=1)
+                bands = jnp.concatenate([bands, f_low[g, :, span], bands], axis=1)
+                total = total + dot(waves, bands, 1, 1)
             real = total[:e_half, :f_half] - total[e_half:, f_half:]
             imag = total[e_half:, :f_half] + total[:e_half, f_half:]
             amp_real[g] = real
@@ -351,7 +371,19 @@
         columns = lax.broadcasted_iota(jnp.int32, (f_half, f_half), 1)
         same = (rows // GROUP == columns // GROUP).astype(F32)
         shells = dot(total, same, 1, 0, lax.Precision.HIGHEST) / (all_slots * M * replicas)
-        coefficient = shell_ref[2] * shell_ref[1] * (shells - shell_ref[0])
+        count_shells = coarse * fine
+        shell = lax.broadcasted_iota(jnp.int32, (8, count_shells), 1)
+        in_row = shell // fine == lax.broadcasted_iota(jnp.int32, (8, count_shells), 0)
+        shell = lax.broadcasted_iota(jnp.int32, (count_shells, f_half), 0)
+        in_lane = shell % fine == lax.broadcasted_iota(jnp.int32, (count_shells, f_half), 1) // GROUP
+
+        def spread(values):
+            rows = jnp.where(in_row, values, 0.0)
+            return dot(rows, in_lane.astype(F32), 1, 0, lax.Precision.HIGHEST)
+
+        order = lax.broadcasted_iota(jnp.int32, (1, count_shells), 1).astype(F32)
+        gain = precision_ref[...] * (1.0 + q_step * order) * (2.0 / (M * math.sqrt(all_slots)))
+        coefficient = spread(gain) * (shells - spread(target_ref[...]))
         wide = jnp.concatenate(
             [jnp.broadcast_to(coefficient[a : a + 1], (GROUP, f_half)) for a in range(coarse)], axis=0
         )
@@ -368,13 +400,12 @@
                 [jnp.concatenate([real, imag], axis=1), jnp.concatenate([imag, -real], axis=1)], axis=0
             )
             high, low = split2(mixed)
+            mixed = jnp.concatenate([high, low, high], axis=1)
             directions = table_ref[me, g]
             for part in range(count):
                 span = slice(part * slots, (part + 1) * slots)
-                shells_high = f_high[g, :, span]
-                turned = (
-                    dot(high, shells_high, 1, 0) + dot(low, shells_high, 1, 0) + dot(high, f_low[g, :, span], 1, 0)
-                )
+                bands = f_high[g, :, span]
+                turned = dot(mixed, jnp.concatenate([bands, bands, f_low[g, :, span]], axis=0), 1, 0)
                 waves = e_high[g, :, span].astype(F32) + e_low[g, :, span].astype(F32)
                 force = jnp.zeros((GROUP, slots), F32)
                 for a in range(coarse):
@@ -397,11 +428,10 @@
         for axis in range(3):
             parts = split3(total[axis : axis + 1] * block_hot)
             spread = sum(dot(part.astype(BF16), lanes, 1, 1) for part in parts)
-            for block in range(blocks):
-                mass = mass_ref[:, block * LANES : (block + 1) * LANES]
-                speed[block, axis : axis + 1] += (INNER * TIME_STEP) * mass * spread[block : block + 1]
+            speed[:, axis, :] = speed[:, axis, :] + (INNER * TIME_STEP) * mass_ref[...] * spread
 
     start_halo(0)
+    kick_copies = []
     for outer in range(OUTER):
         first = outer * INNER
         gather_points(first, outer)
@@ -409,15 +439,22 @@
             lambda d: points.at[outer, me], points.at[outer, me], point_send, point_recv, outer, sp_peer, count
         )
         start_all(point_copies)
-        build_own(first)
+        if outer == 0:
+            build_own(first)
+        else:
+            wait_all(kick_copies)
+            apply_kicks(outer - 1)
+            finish_halo(first)
+            build_halo(first)
         wait_all(point_copies)
         amplitudes(outer)
         sp_copies = group_copies(
             lambda d: level_sp.at[outer, me], level_sp.at[outer, me], sp_send, sp_recv, outer, sp_peer, count
         )
         start_all(sp_copies)
-        finish_halo(first)
-        build_halo(first)
+        if outer == 0:
+            finish_halo(first)
+            build_halo(first)
         wait_all(sp_copies)
         total = level_sp[outer, 0]
         for k in range(1, count):
@@ -431,7 +468,6 @@
         for inner in range(1, INNER):
             step = first + inner
             start_halo(step)
-            build_own(step)
             if inner == 1:
                 wait_all(rep_copies)
                 shell_gains(outer)
@@ -452,13 +488,11 @@
             pair_step(step)
         if outer + 1 < OUTER:
             start_halo(first + INNER)
-        wait_all(kick_copies)
-        apply_kicks(outer)
-
-    for block in range(blocks):
-        span = slice(block * LANES, (block + 1) * LANES)
-        pos_out[0, :, span] = states[OUTER * INNER, block, 0:3]
-        vel_out[0, :, span] = speed[block, 0:3]
+    wait_all(kick_copies)
+    apply_kicks(OUTER - 1)
+    for axis in range(3):
+        pos_out[axis] = states[OUTER * INNER, :, axis, :]
+        vel_out[axis] = speed[:, axis, :]
 
 
 def solution(mesh):
@@ -477,22 +511,17 @@
         shells = intensity_exp.shape[0]
         fine = LANES // GROUP
         coarse = shells // fine
-        order = jnp.arange(blocks, dtype=jnp.int32)
-        fourth = jnp.sum(tile_lists[0], axis=-1) - 3 * (order + rim)[None, :]
-        q = 1.0 + 3.0 * jnp.arange(shells, dtype=F32) / shells
-        gain = 2.0 * precision * q / (M * math.sqrt(count * slots))
-        rows = jnp.stack([intensity_exp, gain, jnp.ones_like(q)]).reshape(3, coarse, fine)
-        rows = jnp.pad(jnp.repeat(rows, GROUP, axis=2), ((0, 0), (0, 8 - coarse), (0, 0)))
+        planes = (3, blocks, LANES)
         e_rows, f_rows, wide = 2 * coarse * GROUP, 2 * fine * GROUP, count * slots
         vmem = pl.BlockSpec(memory_space=pltpu.VMEM)
         dma = pltpu.SemaphoreType.DMA
-        return pl.pallas_call(
+        coords, speeds = pl.pallas_call(
             functools.partial(kernel, (count, replicas, blocks, slots, coarse, fine, groups)),
             out_shape=(
-                jax.ShapeDtypeStruct(positions.shape, F32),
-                jax.ShapeDtypeStruct(velocities.shape, F32),
+                jax.ShapeDtypeStruct(planes, F32),
+                jax.ShapeDtypeStruct(planes, F32),
             ),
-            in_specs=[pl.BlockSpec(memory_space=pltpu.SMEM)] + [vmem] * 8,
+            in_specs=[pl.BlockSpec(memory_space=pltpu.SMEM)] + [vmem] * 9,
             out_specs=(vmem, vmem),
             scratch_shapes=[
                 pltpu.VMEM((steps + 1, blocks, 8, LANES), F32),
@@ -501,6 +530,8 @@
                 pltpu.VMEM((blocks, 8, LANES), F32),
                 pltpu.VMEM((blocks, 8, LANES), F32),
                 pltpu.VMEM((2 * blocks, ROWS, LANES), BF16),
+                pltpu.VMEM((2 * blocks, ROWS, LANES), BF16),
+                pltpu.VMEM((blocks, LANES, ROWS), BF16),
                 pltpu.VMEM((blocks, LANES, ROWS), BF16),
                 pltpu.VMEM((OUTER, count, 8, slots), F32),
                 pltpu.VMEM((OUTER, count, 8, LANES), F32),
@@ -531,7 +562,19 @@
                 collective_id=0, has_side_effects=True, vmem_limit_bytes=58 * 1024 * 1024
             ),
             cost_estimate=pl.CostEstimate(flops=40_000_000_000, bytes_accessed=4_000_000, transcendentals=20_000_000),
-        )(fourth, positions, velocities, strength, inv_mass, solute_index, scatter_weight, rows, jnp.asarray(table))
+        )(
+            jnp.transpose(tile_lists[0], (0, 2, 1)),
+            positions.reshape(planes),
+            velocities.reshape(planes),
+            strength.reshape(blocks, LANES),
+            inv_mass.reshape(blocks, LANES),
+            solute_index,
+            scatter_weight,
+            intensity_exp.reshape(1, shells),
+            precision.reshape(1, shells),
+            jnp.asarray(table),
+        )
+        return coords.reshape(positions.shape), speeds.reshape(velocities.shape)
 
     in_specs = (
         P("rep", None, "sp"),

time: 114 us -> 98.4 us (0.86)
  Pallas kernels: 105 us -> 95.4 us
  local copies, waits for them, and re-layouts: 6.36 us -> 2.22 us
  other arithmetic: 1.39 us -> 0 us
    pallas_call x1, Pallas kernels: 105 us -> 95.4 us  [shards(): pl.pallas_call(functools.partial(kernel, (count, replicas, blocks, slots,...]
    pallas_call x2 -> x0, local copies, waits for them, and re-layouts: 2.42 us -> none  [shards(): pl.pallas_call(functools.partial(kernel, (count, replicas, blocks, slots,...]
    unnamed x12 -> x4, local copies, waits for them, and re-layouts: 2.93 us -> 2.22 us
where the time goes in v2:
time: 98.4 us; the launch traced here: 98.2 us
  Pallas kernels  95.4 us (97%)
  local copies, waits for them, and re-layouts  2.22 us (2%)
    pallas_call x1, Pallas kernels, shards(): pl.pallas_call(functools.partial(kernel, (count, replicas, blocks, slots,...  95.4 us
    unnamed x4, local copies, waits for them, and re-layouts  2.22 us

profile of v2, /device:TPU:0, one launch (start us, length us, event | category | flops | bytes accessed | tf_op | source)
XLA Modules:
  0.0 98.2 jit_solution(6855129659985788117)
XLA Ops:
  0.6 95.4 %shard_map.113 = (f32[3,64,128]{2,1,0:T(8,128)}, f32[3,64,128]{2,1,0:T(8,128)}) custom-call(s32[4,4,64]{2,1,0:T(4,128)} %bitcast.17, f32[3,64,128]{2,1,0:T(8,128)} %bitcast.13, f32[3,64,128]{2,1,0:T(8,128)} %bitcast.14, f32[64,128]{1,0:T(8,128)} %bitcast.15, f32[64,128]{1,0:T(8,128)} %bitcast.16, s32[1,256]{1,0:T(1,128)} %solute_ref.1, f32[1,256]{1,0:T(1,128)} %weight_ref.1, ...), custom_call_target="tpu_custom_call" | custom-call | flops 40000000000 | bytes 4000000 | tf_op jit(solution)/shard_map/pallas_call | solution.py:518
  96.0 0.0 copy-start
  96.0 1.6 %copy.18 = f32[1,3,8192]{2,0,1:T(1,128)} copy(f32[1,3,8192]{2,0,1:T(1,128)} %bitcast.12) | data formatting | bytes 196608
  97.6 0.0 copy-done
  97.6 0.6 copy.19
Async XLA Ops:
  96.0 1.6 %copy-start = (f32[3,64,128]{2,1,0:T(8,128)S(1)}, f32[3,64,128]{2,1,0:T(8,128)}, u32[]{:S(2)}) copy-start(f32[3,64,128]{2,1,0:T(8,128)} %get-tuple-element.5) | copy-start | bytes 294916

commit v3 on v2

--- a/solution.py
+++ b/solution.py
@@ -150,12 +150,12 @@
     strength = strength_ref[...]
     push = (TIME_STEP * PAIR_STRENGTH / math.sqrt(4 * LANES)) * strength * mass_ref[...]
     states[0] = jnp.broadcast_to(jnp.where(row == 4, 1.0, 0.0), (blocks, 8, LANES))
-    speed[...] = jnp.zeros_like(speed)
+    speed[0] = jnp.zeros_like(speed[0])
     factor[...] = jnp.zeros_like(factor)
     states[0, :, 3, :] = jnp.log(strength)
     for axis in range(3):
         states[0, :, axis, :] = pos_ref[axis]
-        speed[:, axis, :] = vel_ref[axis]
+        speed[0, :, axis, :] = vel_ref[axis]
         factor[:, axis, :] = push
 
     @pl.when(me == 0)
@@ -256,7 +256,7 @@
             near_features(nears[step % 2], i * chunk, halo_left[step, pl.ds(i * chunk, chunk)])
             near_features(nears[step % 2], rim + blocks + i * chunk, halo_right[step, pl.ds(i * chunk, chunk)])
 
-    def pair_step(step):
+    def pair_block(step):
         near, own = nears[step % 2], owns[step % 2]
         near_next, own_next = nears[(step + 1) % 2], owns[(step + 1) % 2]
 
@@ -272,20 +272,33 @@
                 sums = sums + dot(features[:16], weight, 1, 1)
             sums = sums[:8] + sums[8:]
             state = states[step, block]
-            velocity = speed[block] + factor[block] * (state * sums[4:5] - sums)
-            speed[block] = velocity
+            velocity = speed[step, block] + factor[block] * (state * sums[4:5] - sums)
+            speed[step + 1, block] = velocity
             state = state + TIME_STEP * velocity
             states[step + 1, block] = state
             if step + 1 < OUTER * INNER:
                 near_features(near_next, rim + block, state[None])
                 own_features(own_next, block, state[None])
 
-        unroll = 8 if blocks % 8 == 0 else 1
-
-        @pl.loop(0, blocks // unroll)
+        return one
+
+    def pair_rest(step, done):
+        one = pair_block(step)
+        left = blocks - done
+        unroll = max(k for k in range(1, 9) if left % k == 0)
+
+        @pl.loop(0, left // unroll)
         def _(i):
             for k in range(unroll):
-                one(i * unroll + k)
+                one(done + i * unroll + k)
+
+    def beside(g, parts, part_body, each, step):
+        one = pair_block(step)
+        for k in range(max(parts, each)):
+            if k < parts:
+                part_body(k)
+            if k < each:
+                one(lax.rem(g * each + k, blocks))
 
     slot_index = solute_ref[...]
     pick_block = (lax.broadcasted_iota(jnp.int32, (blocks, slots), 0) == slot_index // LANES)
@@ -304,15 +317,16 @@
             found + [weight_ref[...], jnp.zeros((4, slots), F32)], axis=0
         )
 
-    def amplitudes(outer):
+    def amplitudes(outer, step, each):
         level[...] = jnp.zeros_like(level)
         width = slots
 
         @pl.loop(0, groups)
         def _(g):
             directions = table_ref[me, g]
-            total = jnp.zeros((2 * e_half, 2 * f_half), F32)
-            for part in range(count):
+            totals = [jnp.zeros((2 * e_half, 2 * f_half), F32)]
+
+            def one_part(part):
                 span = slice(part * width, (part + 1) * width)
                 spot = points[outer, part]
                 project = (
@@ -346,7 +360,10 @@
                 waves, bands = e_high[g, :, span], f_high[g, :, span]
                 waves = jnp.concatenate([waves, waves, e_low[g, :, span]], axis=1)
                 bands = jnp.concatenate([bands, f_low[g, :, span], bands], axis=1)
-                total = total + dot(waves, bands, 1, 1)
+                totals[0] = totals[0] + dot(waves, bands, 1, 1)
+
+            beside(g, count, one_part, each, step)
+            total = totals[0]
             real = total[:e_half, :f_half] - total[e_half:, f_half:]
             imag = total[e_half:, :f_half] + total[:e_half, f_half:]
             amp_real[g] = real
@@ -389,7 +406,7 @@
         )
         gains[...] = jnp.where(diagonal_mask(), wide, 0.0)
 
-    def kicks(outer):
+    def kicks(outer, step, each):
         kick_sum[...] = jnp.zeros_like(kick_sum)
 
         @pl.loop(0, groups)
@@ -402,7 +419,7 @@
             high, low = split2(mixed)
             mixed = jnp.concatenate([high, low, high], axis=1)
             directions = table_ref[me, g]
-            for part in range(count):
+            def one_part(part):
                 span = slice(part * slots, (part + 1) * slots)
                 bands = f_high[g, :, span]
                 turned = dot(mixed, jnp.concatenate([bands, bands, f_low[g, :, span]], axis=0), 1, 0)
@@ -415,12 +432,14 @@
                 for axis in range(3):
                     kick_sum[axis, :, span] += directions[:, axis : axis + 1] * force
 
+            beside(g, count, one_part, each, step)
+
         for part in range(count):
             span = slice(part * slots, (part + 1) * slots)
             sums = [-jnp.sum(kick_sum[axis, :, span], axis=0, keepdims=True) for axis in range(3)]
             kick_out[outer, part] = jnp.concatenate(sums + [jnp.zeros((5, slots), F32)], axis=0)
 
-    def apply_kicks(outer):
+    def apply_kicks(outer, step):
         total = kick_in[outer, 0]
         for k in range(1, count):
             total = total + kick_in[outer, k]
@@ -428,7 +447,7 @@
         for axis in range(3):
             parts = split3(total[axis : axis + 1] * block_hot)
             spread = sum(dot(part.astype(BF16), lanes, 1, 1) for part in parts)
-            speed[:, axis, :] = speed[:, axis, :] + (INNER * TIME_STEP) * mass_ref[...] * spread
+            speed[step, :, axis, :] = speed[step, :, axis, :] + (INNER * TIME_STEP) * mass_ref[...] * spread
 
     start_halo(0)
     kick_copies = []
@@ -443,18 +462,18 @@
             build_own(first)
         else:
             wait_all(kick_copies)
-            apply_kicks(outer - 1)
-            finish_halo(first)
-            build_halo(first)
+            apply_kicks(outer - 1, first)
+        finish_halo(first)
+        build_halo(first)
         wait_all(point_copies)
-        amplitudes(outer)
+        each = blocks // (groups + 3)
+        amplitudes(outer, first, each)
         sp_copies = group_copies(
             lambda d: level_sp.at[outer, me], level_sp.at[outer, me], sp_send, sp_recv, outer, sp_peer, count
         )
         start_all(sp_copies)
-        if outer == 0:
-            finish_halo(first)
-            build_halo(first)
+        pair_rest(first, each * groups)
+        start_halo(first + 1)
         wait_all(sp_copies)
         total = level_sp[outer, 0]
         for k in range(1, count):
@@ -464,35 +483,34 @@
             lambda d: level_rep.at[outer, rep], level_rep.at[outer, rep], rep_send, rep_recv, outer, rep_peer, replicas
         )
         start_all(rep_copies)
-        pair_step(first)
-        for inner in range(1, INNER):
-            step = first + inner
+        finish_halo(first + 1)
+        build_halo(first + 1)
+        wait_all(rep_copies)
+        shell_gains(outer)
+        kicks(outer, first + 1, -(-blocks // groups))
+        kick_in[outer, me] = kick_out[outer, me]
+        kick_copies = group_copies(
+            lambda d: kick_out.at[outer, lax.rem(me + d, count)],
+            kick_in.at[outer, me],
+            kick_send,
+            kick_recv,
+            outer,
+            sp_peer,
+            count,
+        )
+        start_all(kick_copies)
+        for step in range(first + 2, first + INNER):
             start_halo(step)
-            if inner == 1:
-                wait_all(rep_copies)
-                shell_gains(outer)
-                kicks(outer)
-                kick_in[outer, me] = kick_out[outer, me]
-                kick_copies = group_copies(
-                    lambda d: kick_out.at[outer, lax.rem(me + d, count)],
-                    kick_in.at[outer, me],
-                    kick_send,
-                    kick_recv,
-                    outer,
-                    sp_peer,
-                    count,
-                )
-                start_all(kick_copies)
             finish_halo(step)
             build_halo(step)
-            pair_step(step)
+            pair_rest(step, 0)
         if outer + 1 < OUTER:
             start_halo(first + INNER)
     wait_all(kick_copies)
-    apply_kicks(OUTER - 1)
+    apply_kicks(OUTER - 1, OUTER * INNER)
     for axis in range(3):
         pos_out[axis] = states[OUTER * INNER, :, axis, :]
-        vel_out[axis] = speed[:, axis, :]
+        vel_out[axis] = speed[OUTER * INNER, :, axis, :]
 
 
 def solution(mesh):
@@ -527,7 +545,7 @@
                 pltpu.VMEM((steps + 1, blocks, 8, LANES), F32),
                 pltpu.VMEM((steps, rim, 8, LANES), F32),
                 pltpu.VMEM((steps, rim, 8, LANES), F32),
-                pltpu.VMEM((blocks, 8, LANES), F32),
+                pltpu.VMEM((steps + 1, blocks, 8, LANES), F32),
                 pltpu.VMEM((blocks, 8, LANES), F32),
                 pltpu.VMEM((2 * blocks, ROWS, LANES), BF16),
                 pltpu.VMEM((2 * blocks, ROWS, LANES), BF16),

time: 98.4 us -> 118 us (1.20)
  Pallas kernels: 95.4 us -> 115 us
    pallas_call x1, Pallas kernels: 95.4 us -> 115 us  [shards(): pl.pallas_call(functools.partial(kernel, (count, replicas, blocks, slots,...]
where the time goes in v3:
time: 118 us
  Pallas kernels  115 us (97%)
  local copies, waits for them, and re-layouts  2.22 us (2%)
    pallas_call x1, Pallas kernels, shards(): pl.pallas_call(functools.partial(kernel, (count, replicas, blocks, slots,...  115 us

profile of v3, /device:TPU:0, one launch (start us, length us, event | category | flops | bytes accessed | tf_op | source)
XLA Modules:
  0.0 118.3 jit_solution(15610247930320009472)
XLA Ops:
  0.6 115.4 %shard_map.113 = (f32[3,64,128]{2,1,0:T(8,128)}, f32[3,64,128]{2,1,0:T(8,128)}) custom-call(s32[4,4,64]{2,1,0:T(4,128)} %bitcast.17, f32[3,64,128]{2,1,0:T(8,128)} %bitcast.13, f32[3,64,128]{2,1,0:T(8,128)} %bitcast.14, f32[64,128]{1,0:T(8,128)} %bitcast.15, f32[64,128]{1,0:T(8,128)} %bitcast.16, s32[1,256]{1,0:T(1,128)} %solute_ref.1, f32[1,256]{1,0:T(1,128)} %weight_ref.1, ...), custom_call_target="tpu_custom_call" | custom-call | flops 40000000000 | bytes 4000000 | tf_op jit(solution)/shard_map/pallas_call | solution.py:536
  116.1 0.0 copy-start
  116.1 1.6 %copy.18 = f32[1,3,8192]{2,0,1:T(1,128)} copy(f32[1,3,8192]{2,0,1:T(1,128)} %bitcast.12) | data formatting | bytes 196608
  117.6 0.0 copy-done
  117.6 0.6 copy.19
Async XLA Ops:
  116.1 1.6 %copy-start = (f32[3,64,128]{2,1,0:T(8,128)S(1)}, f32[3,64,128]{2,1,0:T(8,128)}, u32[]{:S(2)}) copy-start(f32[3,64,128]{2,1,0:T(8,128)} %get-tuple-element.5) | copy-start | bytes 294916

commit v4 on v2

--- a/solution.py
+++ b/solution.py
@@ -260,32 +260,49 @@
         near, own = nears[step % 2], owns[step % 2]
         near_next, own_next = nears[(step + 1) % 2], owns[(step + 1) % 2]
 
-        def one(block):
-            fourth = tile_ref[step, 0, block] + tile_ref[step, 1, block] + tile_ref[step, 2, block]
-            fourth = fourth + tile_ref[step, 3, block] - 3 * (block + rim)
-            fourth = jnp.clip(fourth, 0, 2 * blocks - 1)
-            mine = own[block]
-            sums = jnp.zeros((16, LANES), F32)
-            for pair in ((block, block + rim), (block + 2 * rim, fourth)):
-                features = jnp.concatenate([near[pair[0]], near[pair[1]]], axis=1)
-                weight = jnp.exp(dot(mine, features, 1, 0)).astype(BF16)
-                sums = sums + dot(features[:16], weight, 1, 1)
-            sums = sums[:8] + sums[8:]
-            state = states[step, block]
-            velocity = speed[block] + factor[block] * (state * sums[4:5] - sums)
-            speed[block] = velocity
-            state = state + TIME_STEP * velocity
-            states[step + 1, block] = state
-            if step + 1 < OUTER * INNER:
-                near_features(near_next, rim + block, state[None])
-                own_features(own_next, block, state[None])
-
         unroll = 8 if blocks % 8 == 0 else 1
 
         @pl.loop(0, blocks // unroll)
         def _(i):
+            start = i * unroll
+            sides = []
             for k in range(unroll):
-                one(i * unroll + k)
+                block = start + k
+                fourth = tile_ref[step, 0, block] + tile_ref[step, 1, block] + tile_ref[step, 2, block]
+                fourth = fourth + tile_ref[step, 3, block] - 3 * (block + rim)
+                fourth = jnp.clip(fourth, 0, 2 * blocks - 1)
+                sides.append(((block, block + rim), (block + 2 * rim, fourth)))
+
+            def weigh(k):
+                mine = own[start + k]
+                found = []
+                for pair in sides[k]:
+                    features = jnp.concatenate([near[pair[0]], near[pair[1]]], axis=1)
+                    found.append((features[:16], jnp.exp(dot(mine, features, 1, 0)).astype(BF16)))
+                return found
+
+            def add_up(found):
+                sums = jnp.zeros((16, LANES), F32)
+                for features, weight in found:
+                    sums = sums + dot(features, weight, 1, 1)
+                return sums[:8] + sums[8:]
+
+            sums, held = [], weigh(0)
+            for k in range(1, unroll):
+                ahead = weigh(k)
+                sums.append(add_up(held))
+                held = ahead
+            sums.append(add_up(held))
+            sums = jnp.stack(sums)
+            here = pl.ds(start, unroll)
+            state = states[step, here]
+            velocity = speed[here] + factor[here] * (state * sums[:, 4:5] - sums)
+            speed[here] = velocity
+            state = state + TIME_STEP * velocity
+            states[step + 1, here] = state
+            if step + 1 < OUTER * INNER:
+                near_features(near_next, rim + start, state)
+                own_features(own_next, start, state)
 
     slot_index = solute_ref[...]
     pick_block = (lax.broadcasted_iota(jnp.int32, (blocks, slots), 0) == slot_index // LANES)

time: 98.4 us -> 98.5 us (level)
  no operation moved by 1% of the time
where the time goes in v4:
time: 98.5 us; the launch traced here: 98.4 us
  Pallas kernels  95.5 us (97%)
  local copies, waits for them, and re-layouts  2.22 us (2%)
    pallas_call x1, Pallas kernels, shards(): pl.pallas_call(functools.partial(kernel, (count, replicas, blocks, slots,...  95.5 us
    unnamed x4, local copies, waits for them, and re-layouts  2.22 us

profile of v4, /device:TPU:0, one launch (start us, length us, event | category | flops | bytes accessed | tf_op | source)
XLA Modules:
  0.0 98.4 jit_solution(13570048046465140998)
XLA Ops:
  0.6 95.5 %shard_map.113 = (f32[3,64,128]{2,1,0:T(8,128)}, f32[3,64,128]{2,1,0:T(8,128)}) custom-call(s32[4,4,64]{2,1,0:T(4,128)} %bitcast.17, f32[3,64,128]{2,1,0:T(8,128)} %bitcast.13, f32[3,64,128]{2,1,0:T(8,128)} %bitcast.14, f32[64,128]{1,0:T(8,128)} %bitcast.15, f32[64,128]{1,0:T(8,128)} %bitcast.16, s32[1,256]{1,0:T(1,128)} %solute_ref.1, f32[1,256]{1,0:T(1,128)} %weight_ref.1, ...), custom_call_target="tpu_custom_call" | custom-call | flops 40000000000 | bytes 4000000 | tf_op jit(solution)/shard_map/pallas_call | solution.py:535
  96.1 0.0 copy-start
  96.1 1.6 %copy.18 = f32[1,3,8192]{2,0,1:T(1,128)} copy(f32[1,3,8192]{2,0,1:T(1,128)} %bitcast.12) | data formatting | bytes 196608
  97.7 0.0 copy-done
  97.7 0.6 copy.19
Async XLA Ops:
  96.1 1.6 %copy-start = (f32[3,64,128]{2,1,0:T(8,128)S(1)}, f32[3,64,128]{2,1,0:T(8,128)}, u32[]{:S(2)}) copy-start(f32[3,64,128]{2,1,0:T(8,128)} %get-tuple-element.5) | copy-start | bytes 294916
